TPU v7x, 32 devices: a whole 2x2x4 slice. The times are simulated.
32 devices in a mesh: kv: 2 (over y), key: 4 (over z), tok: 4 (over x, core).
Axes of the slice: x: 2, y: 2, z: 4, core: 2. Of those that a mesh axis runs over, the one named last changes fastest.
Arguments:
- queries: bfloat16 [1024, 8192], P('key', ('kv', 'tok')), may hold values from -200 to 200
- keys: bfloat16 [1024, 1024], P('key', 'kv'), may hold values from -8 to 8
- values: bfloat16 [1024, 1024], P('key', 'kv'), may hold values from -6 to 6
- doc_ids: int32 [1024], replicated, may hold values from 0 to 5, never falling along the last dimension, each value on 1 to 512 neighbouring positions
- out_weight: bfloat16 [8192, 8192], P('kv', 'tok'), may hold values from -0.0625 to 0.0625
Outputs:
- mixed: bfloat16 [1024, 8192], P(('key', 'kv'), 'tok')
Inputs may be any that keep to these rules, and one draw needn't show every extreme that they name: `doc_ids`: document numbers never fall along the window; a document covers at most 512 positions and some document covers exactly that many.
All inputs are finite; a program needn't handle non-finite values.
Results may differ from a plain program's by a relative error of at most 0.014.
Values may be sent and summed in bfloat16 or wider, within the bound.
A program may use at most 64 MiB of HBM per device.

v0:
```python
import math

import jax
import jax.numpy as jnp
from jax import lax
from jax.sharding import PartitionSpec as P

QUERY_HEADS = 64
KEY_VALUE_HEADS = 8
HEAD_SIZE = 128


very_low = -1e30


def from_behind(block, axis, distance):
    devices = range(lax.axis_size(axis))
    route = [(i - distance, i) for i in devices if i - distance in devices]
    return lax.ppermute(block, axis, route)


def reaches(doc_ids, query_range, key_range, row_count):
    last_key = lax.dynamic_slice_in_dim(doc_ids, key_range * row_count + row_count - 1, 1)[0]
    first_query = lax.dynamic_slice_in_dim(doc_ids, query_range * row_count, 1)[0]
    return (query_range == key_range) | (query_range > key_range) & (last_key == first_query)


def attend(query_block, query_start, key_block, value_block, key_start, doc_ids, tok_index, active):
    row_count = query_block.shape[0]
    key_count = key_block.shape[0]
    head_count = query_block.shape[1] // HEAD_SIZE
    kv_count = key_block.shape[1] // HEAD_SIZE
    group_width = QUERY_HEADS // KEY_VALUE_HEADS
    kv_local = (tok_index * head_count + jnp.arange(head_count, dtype=jnp.int32)) // group_width
    selector = (jnp.arange(kv_count, dtype=jnp.int32)[None, :] == kv_local[:, None]).astype(
        jnp.bfloat16
    )

    def compute(unused):
        query_three = query_block.reshape(row_count, head_count, HEAD_SIZE)
        key_sel = jnp.einsum(
            "skd,hk->shd",
            key_block.reshape(key_count, kv_count, HEAD_SIZE),
            selector,
            preferred_element_type=jnp.float32,
        ).astype(jnp.bfloat16)
        value_sel = jnp.einsum(
            "skd,hk->shd",
            value_block.reshape(key_count, kv_count, HEAD_SIZE),
            selector,
            preferred_element_type=jnp.float32,
        ).astype(jnp.bfloat16)
        scores = jnp.einsum(
            "qhd,shd->hqs", query_three, key_sel, preferred_element_type=jnp.float32
        ) * (1.0 / math.sqrt(HEAD_SIZE))
        query_docs = lax.dynamic_slice_in_dim(doc_ids, query_start, row_count)
        key_docs = lax.dynamic_slice_in_dim(doc_ids, key_start, key_count)
        query_pos = query_start + jnp.arange(row_count, dtype=jnp.int32)
        key_pos = key_start + jnp.arange(key_count, dtype=jnp.int32)
        allowed = (query_docs[:, None] == key_docs[None, :]) & (
            key_pos[None, :] <= query_pos[:, None]
        )
        highest = jnp.max(jnp.where(allowed[None], scores, very_low), axis=2)
        weights = jnp.exp(jnp.where(allowed[None], scores - highest[:, :, None], very_low))
        totals = jnp.sum(weights, axis=2).T
        weighted = jnp.einsum(
            "hqs,shd->qhd",
            weights.astype(jnp.bfloat16),
            value_sel,
            preferred_element_type=jnp.float32,
        )
        positive = totals > 0
        safe = jnp.where(positive, totals, 1.0)
        piece = (
            (weighted / safe[:, :, None])
            .astype(jnp.bfloat16)
            .reshape(row_count, head_count * HEAD_SIZE)
        )
        log_total = jnp.where(positive, highest.T + jnp.log(safe), very_low)
        return (piece, log_total)

    def skipped(unused):
        return (
            jnp.zeros((row_count, head_count * HEAD_SIZE), jnp.bfloat16),
            jnp.full((row_count, head_count), very_low, jnp.float32),
        )

    return lax.cond(active, compute, skipped, 0)


def merge(pieces, log_totals):
    slots, row_count, width = pieces.shape
    head_count = log_totals.shape[2]
    top = jnp.max(log_totals, axis=0)
    factors = jnp.exp(log_totals - top[None])
    numerator = jnp.sum(
        factors[..., None]
        * pieces.reshape(slots, row_count, head_count, HEAD_SIZE).astype(jnp.float32),
        axis=0,
    )
    denominator = jnp.sum(factors, axis=0)
    return (numerator / denominator[..., None]).astype(jnp.bfloat16).reshape(row_count, width)


def per_device(queries, keys, values, doc_ids, out_weight):
    key_count = lax.axis_size("key")
    key_index = lax.axis_index("key")
    tok_index = lax.axis_index("tok")
    row_count = queries.shape[0]
    own_start = key_index * row_count
    reach_count = key_count // 2
    own_piece, own_total = attend(
        queries, own_start, keys, values, own_start, doc_ids, tok_index, jnp.array(True)
    )
    piece_list = [own_piece]
    total_list = [own_total]
    for offset in range(1, reach_count + 1):
        earlier_keys, earlier_values = from_behind((keys, values), "key", offset)
        target = key_index - offset
        active = (target >= 0) & reaches(doc_ids, key_index, jnp.maximum(target, 0), row_count)
        result = attend(
            queries,
            own_start,
            earlier_keys,
            earlier_values,
            target * row_count,
            doc_ids,
            tok_index,
            active,
        )
        piece_list.append(result[0])
        total_list.append(result[1])
    pieces = jnp.stack(piece_list)
    log_totals = jnp.stack(total_list)
    attn = merge(pieces, log_totals)
    total = jnp.dot(
        lax.all_gather(attn, "tok", axis=1, tiled=True),
        out_weight,
        preferred_element_type=jnp.float32,
    )
    return lax.psum_scatter(total.astype(jnp.bfloat16), "kv", scatter_dimension=0, tiled=True)


def solution(mesh):
    placed = (P("key", ("kv", "tok")), P("key", "kv"), P("key", "kv"), P(), P("kv", "tok"))
    return jax.shard_map(
        per_device, mesh=mesh, in_specs=placed, out_specs=P(("key", "kv"), "tok"), check_vma=False
    )
```

profile of v0, /device:TPU:0, one launch (start us, length us, event | category | flops | bytes accessed | tf_op | source)
XLA Modules:
  0.0 119.8 jit_solution(4947111507803305670)
XLA Ops:
  6.5 0.0 all-gather.2.cloned.1.call-start
  6.5 6.6 %collective-permute-start.2 = (bf16[256,512]{1,0:T(8,128)(2,1)}, bf16[256,512]{1,0:T(8,128)(2,1)}, u32[]{:S(2)}, u32[]{:S(2)}) collective-permute-start(bf16[256,512]{1,0:T(8,128)(2,1)} %param.11), channel_id=1, source_target_pairs={{0,8},{4,12},{1,9},{5,13},{2,10},{6,14},{3,11},{7,15},{16,24},{20,... | collective-permute-start | bytes 786440 | tf_op jit(solution)/shard_map/ppermute | solution.py:19
  13.2 4.2 %collective-permute-start = (bf16[256,512]{1,0:T(8,128)(2,1)}, bf16[256,512]{1,0:T(8,128)(2,1)}, u32[]{:S(2)}, u32[]{:S(2)}) collective-permute-start(bf16[256,512]{1,0:T(8,128)(2,1)} %param.11), channel_id=1, source_target_pairs={{0,4},{4,8},{8,12},{1,5},{5,9},{9,13},{2,6},{6,10},{10,14},{3,7},{... | collective-permute-start | bytes 786440 | tf_op jit(solution)/shard_map/ppermute | solution.py:19
  17.4 2.0 %collective-permute-start.3 = (bf16[256,512]{1,0:T(8,128)(2,1)}, bf16[256,512]{1,0:T(8,128)(2,1)}, u32[]{:S(2)}, u32[]{:S(2)}) collective-permute-start(bf16[256,512]{1,0:T(8,128)(2,1)} %param.10), channel_id=1, source_target_pairs={{0,8},{4,12},{1,9},{5,13},{2,10},{6,14},{3,11},{7,15},{16,24},{20,... | collective-permute-start | bytes 786440 | tf_op jit(solution)/shard_map/ppermute | solution.py:19
  19.3 2.0 %collective-permute-start.1 = (bf16[256,512]{1,0:T(8,128)(2,1)}, bf16[256,512]{1,0:T(8,128)(2,1)}, u32[]{:S(2)}, u32[]{:S(2)}) collective-permute-start(bf16[256,512]{1,0:T(8,128)(2,1)} %param.10), channel_id=1, source_target_pairs={{0,4},{4,8},{8,12},{1,5},{5,9},{9,13},{2,6},{6,10},{10,14},{3,7},{... | collective-permute-start | bytes 786440 | tf_op jit(solution)/shard_map/ppermute | solution.py:19
  21.3 1.0 reshape.348
  22.4 1.0 reshape.350
  23.4 0.8 dynamic_slice.34
  24.2 0.1 compare_and_fusion.2
  24.3 0.3 fusion.80
  24.7 1.5 %fusion.54 = (f32[8,256]{1,0:T(8,128)S(1)}, f32[8,256,256]{2,1,0:T(8,128)S(1)}) fusion(pred[256,256]{0,1:T(8,128)(4,1)S(1)} %compare_and_fusion.2, bf16[8,256,128]{2,0,1:T(8,128)(2,1)S(1)} %fusion.80, bf16[256,1024]{1,0:T(8,128)(2,1)} %param.9), kind=kOutput, calls=%fused_computation.74 | convolution fusion | flops 135788544 | bytes 3219456 | tf_op jit(solution)/shard_map/cond/branch_1_fun/qhd,shd->hqs/dot_general | solution.py:53
  26.2 0.4 fusion.58
  26.7 0.3 fusion.78
  27.1 0.3 copy.25
  27.4 0.0 copy-start
  27.4 1.4 %fusion.61 = bf16[1,256,8,128]{1,3,2,0:T(8,128)(2,1)} fusion(f32[8,256,256]{2,1,0:T(8,128)S(1)} %get-tuple-element.137, f32[8,256]{1,0:T(8,128)S(1)} %get-tuple-element.136, pred[256,256]{0,1:T(8,128)(4,1)S(1)} %compare_and_fusion.2, f32[256,8]{0,1:T(8,128)S(1)} %compare_select_fusion.5, bf16[8,256,128]{1,2,0:T(8,128)(2,1)S(1)} %copy.25), kind=kOutput, calls=%fused_computation.82 | convolution fusion | flops 136839168 | bytes 3227648 | tf_op jit(solution)/shard_map/cond/branch_1_fun/hqs,shd->qhd/dot_general | solution.py:66
  28.8 0.0 copy-done
  28.8 0.7 fusion.91
  32.1 0.0 collective-permute-done.2
  32.1 0.0 collective-permute-done.3
  32.1 0.1 conditional.3
  32.2 0.0 collective-permute-done
  32.2 3.1 %collective-permute-done.1 = bf16[256,512]{1,0:T(8,128)(2,1)} collective-permute-done((bf16[256,512]{1,0:T(8,128)(2,1)}, bf16[256,512]{1,0:T(8,128)(2,1)}, u32[]{:S(2)}, u32[]{:S(2)}) %collective-permute-start.1) | collective-permute-done | bytes 262176 | tf_op jit(solution)/shard_map/ppermute | solution.py:19
  35.3 0.1 conditional.2
  35.4 1.5 %multiply_reduce_fusion = f32[256,8,128]{0,2,1:T(8,128)S(1)} fusion(bf16[1,256,8,128]{1,3,2,0:T(8,128)(2,1)S(1)} %get-tuple-element.110, bf16[1,256,8,128]{1,3,2,0:T(8,128)(2,1)S(1)} %get-tuple-element.109, bf16[1,256,8,128]{1,3,2,0:T(8,128)(2,1)} %fusion.61, f32[3,256,8]{1,2,0:T(8,128)S(1)} %get-tuple-element.116), kind=kLoop, calls=%fused_computation.70 | loop fusion | flops 3670016 | bytes 2646016 | tf_op jit(solution)/shard_map/reduce_sum | solution.py:96
  36.9 0.9 divide_convert_fusion
  37.8 0.0 all-gather.2.cloned.1.call-update
  37.8 0.2 reduce-scatter.2.cloned.1.call-start
  38.1 42.5 %all-gather.2.cloned.1.call-done = bf16[256,4096]{0,1:T(8,128)(2,1)} async-done(((bf16[256,1024]{0,1:T(8,128)(2,1)}), bf16[256,4096]{0,1:T(8,128)(2,1)}) %all-gather.2.cloned.1.call-update) | async-done | bytes 2097168 | tf_op jit(solution)/shard_map/all_gather | solution.py:137
  80.5 11.9 %convolution_convert_fusion = bf16[256,2048]{1,0:T(8,128)(2,1)} fusion(bf16[256,4096]{0,1:T(8,128)(2,1)} %all-gather.2.cloned.1.call-done, bf16[4096,2048]{1,0:T(8,128)(2,1)} %param.13), kind=kOutput, calls=%fused_computation.71 | convolution fusion | flops 4295491584 | bytes 19922944 | tf_op jit(solution)/shard_map/dot_general | solution.py:136
  92.4 0.0 reduce-scatter.2.cloned.1.call-update
  92.5 20.5 %reduce-scatter.2.cloned.1.call-done = bf16[128,2048]{1,0:T(8,128)(2,1)} async-done(((bf16[256,2048]{1,0:T(8,128)(2,1)}), bf16[128,2048]{1,0:T(8,128)(2,1)}) %reduce-scatter.2.cloned.1.call-update) | async-done | bytes 524304 | tf_op jit(solution)/shard_map/reduce_scatter | solution.py:141
  (10 shorter events, 0.1 us)
Async XLA Ops:
  6.5 74.0 %all-gather.2.cloned.1.call-start = ((), (), s32[]{:S(2)}) async-start(), calls=%async_computation.1 | async-start | bytes 2621440 | tf_op jit(solution)/shard_map/all_gather | solution.py:137
  6.5 25.6 %collective-permute-start.2 = (bf16[256,512]{1,0:T(8,128)(2,1)}, bf16[256,512]{1,0:T(8,128)(2,1)}, u32[]{:S(2)}, u32[]{:S(2)}) collective-permute-start(bf16[256,512]{1,0:T(8,128)(2,1)} %param.11), channel_id=1, source_target_pairs={{0,8},{4,12},{1,9},{5,13},{2,10},{6,14},{3,11},{7,15},{16,24},{20,... | collective-permute-start | bytes 786440 | tf_op jit(solution)/shard_map/ppermute | solution.py:19
  13.2 19.0 %collective-permute-start = (bf16[256,512]{1,0:T(8,128)(2,1)}, bf16[256,512]{1,0:T(8,128)(2,1)}, u32[]{:S(2)}, u32[]{:S(2)}) collective-permute-start(bf16[256,512]{1,0:T(8,128)(2,1)} %param.11), channel_id=1, source_target_pairs={{0,4},{4,8},{8,12},{1,5},{5,9},{9,13},{2,6},{6,10},{10,14},{3,7},{... | collective-permute-start | bytes 786440 | tf_op jit(solution)/shard_map/ppermute | solution.py:19
  17.4 14.8 %collective-permute-start.3 = (bf16[256,512]{1,0:T(8,128)(2,1)}, bf16[256,512]{1,0:T(8,128)(2,1)}, u32[]{:S(2)}, u32[]{:S(2)}) collective-permute-start(bf16[256,512]{1,0:T(8,128)(2,1)} %param.10), channel_id=1, source_target_pairs={{0,8},{4,12},{1,9},{5,13},{2,10},{6,14},{3,11},{7,15},{16,24},{20,... | collective-permute-start | bytes 786440 | tf_op jit(solution)/shard_map/ppermute | solution.py:19
  19.3 15.9 %collective-permute-start.1 = (bf16[256,512]{1,0:T(8,128)(2,1)}, bf16[256,512]{1,0:T(8,128)(2,1)}, u32[]{:S(2)}, u32[]{:S(2)}) collective-permute-start(bf16[256,512]{1,0:T(8,128)(2,1)} %param.10), channel_id=1, source_target_pairs={{0,4},{4,8},{8,12},{1,5},{5,9},{9,13},{2,6},{6,10},{10,14},{3,7},{... | collective-permute-start | bytes 786440 | tf_op jit(solution)/shard_map/ppermute | solution.py:19
  27.4 1.5 %copy-start = (s32[1024]{0:T(1024)S(1)}, s32[1024]{0:T(1024)}, u32[]{:S(2)}) copy-start(s32[1024]{0:T(1024)} %param.12) | copy-start | bytes 12292
  37.8 75.1 %reduce-scatter.2.cloned.1.call-start = ((), (), s32[]{:S(2)}) async-start(), calls=%async_computation.2 | async-start | bytes 1572864 | tf_op jit(solution)/shard_map/reduce_scatter | solution.py:141
Sparse Core Ops, SparseCore 0:
  37.9 42.5 all-gather.1
  92.6 20.3 reduce-scatter.1
where the time goes:
time: 121 us; the launch traced here: 120 us
  waiting for transfers between devices  66.1 us (55%)
  between operations  16.2 us (13%)
  matrix products  15.6 us (13%)
  starting transfers between devices  15 us (12%)
  local copies, waits for them, and re-layouts  3.86 us (3%)
  other arithmetic  3.05 us (3%)
    all_gather x1, waiting for transfers between devices, per_device(): lax.all_gather(attn, 'tok', axis=1, tiled=True)  42.5 us
    reduce_scatter x1, waiting for transfers between devices, per_device(): lax.psum_scatter(total.astype(jnp.bfloat16), 'kv', scatter_dimension=0, t...  20.5 us
    ppermute x4, starting transfers between devices, from_behind(): return lax.ppermute(block, axis, route)  14.8 us
    dot_general x1, matrix products, per_device(): jnp.dot(lax.all_gather(attn, 'tok', axis=1, tiled=True), out_weight, pref...  11.9 us
    ppermute x4, waiting for transfers between devices, from_behind(): return lax.ppermute(block, axis, route)  3.07 us
  transfers between devices with their start and end apart: 6, of which 3 were waited for; matrix products, arithmetic and copies ran while one was open for 7% of the time, Pallas kernels for 0%

commit v1 on v0

v1 whole, which is shorter than its diff:
```python
import functools
import math

import jax
import jax.numpy as jnp
from jax import lax
from jax.experimental import pallas as pl
from jax.experimental.pallas import tpu as pltpu
from jax.sharding import PartitionSpec as P

QUERY_HEADS = 64
KEY_VALUE_HEADS = 8
HEAD_SIZE = 128

very_low = -1e30
MESH = pl.DeviceIdType.MESH


def kernel(dims, doc_ref, q_hbm, k_hbm, v_hbm, w_hbm, out_ref,
           qs, kvbuf, wv, acc, mx, gath, psend, rbuf, own,
           load_sem, w_sem, zs, zr, gs, gr, ys, yr):
    n_key, n_tok, n_kv, reach, heads, rows, ch, sub, n_col, ct = dims
    xs = n_tok // 2
    block = ch * sub
    n_ch = n_kv * sub
    group = QUERY_HEADS // KEY_VALUE_HEADS
    key = lax.axis_index("key")
    tok = lax.axis_index("tok")
    kv = lax.axis_index("kv")
    tx, core = tok // 2, tok % 2
    mate = tx * 2 + (1 - core)
    kv_local = (tok * heads) // group
    has_next = key + 1 < n_key

    barrier = pltpu.get_barrier_semaphore()

    def greet(where):
        pl.semaphore_signal(barrier, inc=1, device_id=where, device_id_type=MESH)

    @pl.when(key > 0)
    def _():
        greet({"key": key - 1})

    @pl.when(has_next)
    def _():
        greet({"key": key + 1})

    greet({"tok": mate})
    for d in range(1, xs):
        greet({"tok": ((tx + d) % xs) * 2 + core})
    for d in range(1, n_kv):
        greet({"kv": (kv + d) % n_kv})

    cols = pl.ds(pl.multiple_of(kv_local * HEAD_SIZE, HEAD_SIZE), HEAD_SIZE)
    kload = pltpu.make_async_copy(k_hbm.at[:, cols], kvbuf.at[0, 0], load_sem.at[0])
    vload = pltpu.make_async_copy(v_hbm.at[:, cols], kvbuf.at[0, 1], load_sem.at[1])
    kload.start()
    vload.start()
    qloads = []
    for h in range(heads):
        cp = pltpu.make_async_copy(
            q_hbm.at[:, h * HEAD_SIZE:(h + 1) * HEAD_SIZE], qs.at[h], load_sem.at[2 + h])
        cp.start()
        qloads.append(cp)
    wloads = []
    for n in range(n_col):
        cp = pltpu.make_async_copy(w_hbm.at[:, n * ct:(n + 1) * ct], wv.at[n], w_sem.at[n])
        cp.start()
        wloads.append(cp)
    kload.wait()
    vload.wait()
    greeted = 1 + (xs - 1) + (n_kv - 1)
    pl.semaphore_wait(
        barrier,
        greeted + jnp.where(key > 0, 1, 0) + jnp.where(has_next, 1, 0))

    def zcopy(slot):
        return pltpu.make_async_remote_copy(
            src_ref=kvbuf.at[slot], dst_ref=kvbuf.at[slot + 1],
            send_sem=zs.at[slot], recv_sem=zr.at[slot],
            device_id={"key": key + 1}, device_id_type=MESH)

    @pl.when(has_next)
    def _():
        zcopy(0).start()

    for cp in qloads:
        cp.wait()

    factor = math.log2(math.e) / math.sqrt(HEAD_SIZE)

    def update(r, slot):
        start = pl.multiple_of(r * ch, ch)
        q = qs[:, pl.ds(start, ch), :].reshape(heads * ch, HEAD_SIZE)
        k = kvbuf[slot, 0]
        v = kvbuf[slot, 1]
        s = lax.dot_general(q, k, (((1,), (1,)), ((), ())), preferred_element_type=jnp.float32)
        kdoc = doc_ref[pl.ds(key - slot, 1), :]
        qdoc = doc_ref[pl.ds(key, 1), :]
        at = lax.broadcasted_iota(jnp.int32, (ch, rows), 1)
        row = lax.broadcasted_iota(jnp.int32, (ch, rows), 0) + start
        qcol = jnp.sum(jnp.where(at == row, qdoc, 0), axis=1, keepdims=True)
        allowed = qcol == kdoc
        if slot == 0:
            allowed = allowed & (at <= row)
        bias = jnp.where(allowed, 0.0, very_low)
        s = s.reshape(heads, ch, rows) + bias[None]
        m = jnp.max(s, axis=2, keepdims=True)
        if slot > 0:
            old = mx[r].reshape(heads, ch, HEAD_SIZE)
            m = jnp.maximum(m, old[:, :, :1])
        p = jnp.exp2((s - m) * factor).astype(jnp.bfloat16).reshape(heads * ch, rows)
        ve = jnp.concatenate([v, jnp.ones_like(v)], axis=1)
        pv = jnp.dot(p, ve, preferred_element_type=jnp.float32)
        wide = jnp.broadcast_to(m, (heads, ch, HEAD_SIZE))
        if slot > 0:
            fade = jnp.exp2((old - wide) * factor).reshape(heads * ch, HEAD_SIZE)
            pv = pv + acc[r] * jnp.concatenate([fade, fade], axis=1)
        mx[r] = wide.reshape(heads * ch, HEAD_SIZE)
        acc[r] = pv

    for slot in range(reach):
        @pl.when(key >= slot)
        def _(slot=slot):
            if slot > 0:
                zcopy(slot - 1).wait_recv()

                @pl.when(has_next)
                def _():
                    zcopy(slot).start()
            lax.fori_loop(0, n_ch, lambda r, x: (update(r, slot), x)[1], 0)

    @pl.when(key >= reach)
    def _():
        zcopy(reach - 1).wait_recv()

    def gcopy(c, who, where, sem):
        return pltpu.make_async_remote_copy(
            src_ref=gath.at[c, who], dst_ref=gath.at[c, who],
            send_sem=gs.at[c, sem], recv_sem=gr.at[c, who],
            device_id={"tok": where}, device_id_type=MESH)

    def to_x(c, d):
        return gcopy(c, tok, ((tx + d) % xs) * 2 + core, d - 1)

    def from_x(c, d):
        who = ((tx + d) % xs) * 2 + core
        return gcopy(c, who, who, 0)

    def finish(c):
        r = ((kv + 1 + c // sub) % n_kv) * sub + c % sub

        @pl.when(key >= reach)
        def _():
            update(r, reach)

        a = acc[r]
        o = a[:, :HEAD_SIZE] / a[:, HEAD_SIZE:]
        gath[c, tok] = o.astype(jnp.bfloat16).reshape(heads, ch, HEAD_SIZE)
        for d in range(1, xs):
            to_x(c, d).start()
        gcopy(c, tok, mate, xs - 1).start()

    def forward(c):
        for d in range(1, xs):
            from_x(c, d).wait_recv()
            who = ((tx + d) % xs) * 2 + core
            gcopy(c, who, mate, xs - 1 + d).start()

    def ycopy(c, n):
        d = c // sub + 1
        return pltpu.make_async_remote_copy(
            src_ref=psend.at[c, n], dst_ref=rbuf.at[c, n],
            send_sem=ys.at[c, n], recv_sem=yr.at[c, n],
            device_id={"kv": (kv + d) % n_kv}, device_id_type=MESH)

    n_send = n_ch - sub

    def multiply(c):
        for x in range(xs):
            gcopy(c, x * 2 + (1 - core), mate, 0).wait_recv()
        pieces = [gath[c, t, h] for t in range(n_tok) for h in range(heads)]
        lhs = jnp.concatenate(pieces, axis=1)

        def column(n, x):
            part = jnp.dot(lhs, wv[n], preferred_element_type=jnp.float32)
            if c < n_send:
                psend[c, n] = part.astype(jnp.bfloat16)
                ycopy(c, n).start()
            else:
                own[c - n_send, n] = part
            return x

        lax.fori_loop(0, n_col, column, 0)

    lead = min(2, n_ch - 1)
    for c in range(lead + 1):
        finish(c)
    forward(0)
    for c in range(lead + 1, n_ch):
        finish(c)
    for cp in wloads:
        cp.wait()
    for c in range(n_ch):
        if c + 1 < n_ch and c > 0:
            forward(c + 1)
        multiply(c)
        if c == 0 and n_ch > 1:
            forward(1)

    for s in range(sub):
        for n in range(n_col):
            total = own[s, n]
            for d in range(1, n_kv):
                c = (d - 1) * sub + s
                ycopy(c, n).wait_recv()
                total = total + rbuf[c, n].astype(jnp.float32)
            out_ref[s * ch:(s + 1) * ch, n * ct:(n + 1) * ct] = total.astype(jnp.bfloat16)

    for slot in range(reach):
        @pl.when((key >= slot) & has_next)
        def _(slot=slot):
            zcopy(slot).wait_send()
    for c in range(n_ch):
        for i in range(2 * xs - 1):
            gcopy(c, tok, mate, i).wait_send()
        if c < n_send:
            for n in range(n_col):
                ycopy(c, n).wait_send()


def per_device(sizes, queries, keys, values, doc_ids, out_weight):
    n_kv, n_key, n_tok = sizes
    rows, width = queries.shape
    heads = width // HEAD_SIZE
    depth, features = out_weight.shape
    reach = n_key // 2
    block = rows // n_kv
    sub = 2 if block >= 128 else 1
    ch = block // sub
    n_ch = n_kv * sub
    ct = min(512, features)
    n_col = features // ct
    n_send = n_ch - sub
    dims = (n_key, n_tok, n_kv, reach, heads, rows, ch, sub, n_col, ct)
    bf, f32 = jnp.bfloat16, jnp.float32
    hbm = pl.BlockSpec(memory_space=pl.ANY)
    vmem = pl.BlockSpec(memory_space=pltpu.VMEM)
    dma = pltpu.SemaphoreType.DMA
    flops = 2 * rows * depth * features + 4 * rows * rows * width * (reach + 1)
    return pl.pallas_call(
        functools.partial(kernel, dims),
        out_shape=jax.ShapeDtypeStruct((block, features), bf),
        in_specs=[vmem, hbm, hbm, hbm, hbm],
        out_specs=vmem,
        scratch_shapes=[
            pltpu.VMEM((heads, rows, HEAD_SIZE), bf),
            pltpu.VMEM((reach + 1, 2, rows, HEAD_SIZE), bf),
            pltpu.VMEM((n_col, depth, ct), bf),
            pltpu.VMEM((n_ch, heads * ch, 2 * HEAD_SIZE), f32),
            pltpu.VMEM((n_ch, heads * ch, HEAD_SIZE), f32),
            pltpu.VMEM((n_ch, n_tok, heads, ch, HEAD_SIZE), bf),
            pltpu.VMEM((n_send, n_col, ch, ct), bf),
            pltpu.VMEM((n_send, n_col, ch, ct), bf),
            pltpu.VMEM((sub, n_col, ch, ct), f32),
            dma((2 + heads,)),
            dma((n_col,)),
            dma((reach,)),
            dma((reach,)),
            dma((n_ch, n_tok)),
            dma((n_ch, n_tok)),
            dma((n_send, n_col)),
            dma((n_send, n_col)),
        ],
        compiler_params=pltpu.CompilerParams(
            collective_id=0, has_side_effects=True, vmem_limit_bytes=48 * 1024 * 1024),
        cost_estimate=pl.CostEstimate(
            flops=flops, bytes_accessed=2 * depth * features, transcendentals=0),
    )(doc_ids.reshape(n_key, rows), queries, keys, values, out_weight)


def solution(mesh):
    sizes = tuple(mesh.shape[a] for a in ("kv", "key", "tok"))
    placed = (P("key", ("kv", "tok")), P("key", "kv"), P("key", "kv"), P(), P("kv", "tok"))
    return jax.shard_map(
        functools.partial(per_device, sizes), mesh=mesh, in_specs=placed,
        out_specs=P(("key", "kv"), "tok"), check_vma=False
    )
```

time: 121 us -> 36.6 us (0.30)
  the two profiles are of different devices: /device:TPU:0 before, /device:TPU:17 now
where the time goes in v1:
time: 36.6 us; the launch traced here: 36.4 us
  Pallas kernels  31.9 us (87%)
  local copies, waits for them, and re-layouts  4.43 us (12%)
    pallas_call x1, Pallas kernels, per_device(): pl.pallas_call(functools.partial(kernel, dims), out_shape=jax.ShapeDtypeS...  31.9 us
    unnamed x7, local copies, waits for them, and re-layouts  3.74 us

profile of v1, /device:TPU:17, one launch (start us, length us, event | category | flops | bytes accessed | tf_op | source)
XLA Modules:
  0.0 36.4 jit_solution(8379747026005339237)
XLA Ops:
  0.0 0.7 %reshape.3.doc_ref = s32[4,256]{1,0:T(4,128)S(1)} reshape(s32[1024]{0:T(1024)} %param.8) | data formatting | bytes 8192 | tf_op jit(solution)/shard_map/reshape | solution.py:279
  0.7 0.0 copy-start
  0.7 1.0 %copy-done = bf16[256,1024]{1,0:T(8,128)(2,1)S(1)} copy-done((bf16[256,1024]{1,0:T(8,128)(2,1)S(1)}, bf16[256,1024]{1,0:T(8,128)(2,1)}, u32[]{:S(2)}) %copy-start) | copy-done | bytes 524312
  1.7 0.0 copy-start.1
  1.7 0.9 %copy-done.1 = bf16[256,512]{1,0:T(8,128)(2,1)S(1)} copy-done((bf16[256,512]{1,0:T(8,128)(2,1)S(1)}, bf16[256,512]{1,0:T(8,128)(2,1)}, u32[]{:S(2)}) %copy-start.1) | copy-done | bytes 262168
  2.7 0.0 copy-start.2
  2.7 0.9 %copy-done.2 = bf16[256,512]{1,0:T(8,128)(2,1)S(1)} copy-done((bf16[256,512]{1,0:T(8,128)(2,1)S(1)}, bf16[256,512]{1,0:T(8,128)(2,1)}, u32[]{:S(2)}) %copy-start.2) | copy-done | bytes 262168
  3.6 31.9 %shard_map.55 = bf16[128,2048]{1,0:T(8,128)(2,1)S(1)} custom-call(s32[4,256]{1,0:T(4,128)S(1)} %reshape.3.doc_ref, bf16[256,1024]{1,0:T(8,128)(2,1)S(1)} %copy-done, bf16[256,512]{1,0:T(8,128)(2,1)S(1)} %copy-done.1, bf16[256,512]{1,0:T(8,128)(2,1)S(1)} %copy-done.2, bf16[4096,2048]{1,0:T(8,128)(2,1)} %w_hbm.1), custom_call_target="tpu_custom_call" | custom-call | flops 5100273664 | bytes 16777216 | tf_op jit(solution)/shard_map/pallas_call | solution.py:251
  35.6 0.8 %copy.7 = bf16[128,2048]{1,0:T(8,128)(2,1)} copy(bf16[128,2048]{1,0:T(8,128)(2,1)S(1)} %shard_map.55) | data formatting | bytes 1048576
Async XLA Ops:
  0.7 1.0 %copy-start = (bf16[256,1024]{1,0:T(8,128)(2,1)S(1)}, bf16[256,1024]{1,0:T(8,128)(2,1)}, u32[]{:S(2)}) copy-start(bf16[256,1024]{1,0:T(8,128)(2,1)} %q_hbm.1) | copy-start | bytes 1572868
  1.7 0.9 %copy-start.1 = (bf16[256,512]{1,0:T(8,128)(2,1)S(1)}, bf16[256,512]{1,0:T(8,128)(2,1)}, u32[]{:S(2)}) copy-start(bf16[256,512]{1,0:T(8,128)(2,1)} %k_hbm.1) | copy-start | bytes 786436
  2.7 0.9 %copy-start.2 = (bf16[256,512]{1,0:T(8,128)(2,1)S(1)}, bf16[256,512]{1,0:T(8,128)(2,1)}, u32[]{:S(2)}) copy-start(bf16[256,512]{1,0:T(8,128)(2,1)} %v_hbm.1) | copy-start | bytes 786436

commit v2 on v1

--- a/solution.py
+++ b/solution.py
@@ -176,41 +176,59 @@
 
     n_send = n_ch - sub
 
-    def multiply(c):
-        for x in range(xs):
-            gcopy(c, x * 2 + (1 - core), mate, 0).wait_recv()
-        pieces = [gath[c, t, h] for t in range(n_tok) for h in range(heads)]
-        lhs = jnp.concatenate(pieces, axis=1)
+    width = heads * HEAD_SIZE
+
+    def lhs_of(c, t):
+        return jnp.concatenate([gath[c, t, h] for h in range(heads)], axis=1)
+
+    def near():
+        for c in range(n_ch):
+            gcopy(c, mate, mate, 0).wait_recv()
+        lhs = jnp.concatenate(
+            [jnp.concatenate([lhs_of(c, tx * 2), lhs_of(c, tx * 2 + 1)], axis=1)
+             for c in range(n_ch)], axis=0)
 
         def column(n, x):
-            part = jnp.dot(lhs, wv[n], preferred_element_type=jnp.float32)
-            if c < n_send:
+            w = wv[n, pl.ds(pl.multiple_of(tx * 2 * width, width), 2 * width), :]
+            part = jnp.dot(lhs, w, preferred_element_type=jnp.float32)
+            for c in range(n_ch):
+                own[c, n] = part[c * ch:(c + 1) * ch]
+            return x
+
+        lax.fori_loop(0, n_col, column, 0)
+
+    def far(c, who, last):
+        lhs = lhs_of(c, who)
+
+        def column(n, x):
+            w = wv[n, pl.ds(pl.multiple_of(who * width, width), width), :]
+            part = own[c, n] + jnp.dot(lhs, w, preferred_element_type=jnp.float32)
+            if last and c < n_send:
                 psend[c, n] = part.astype(jnp.bfloat16)
                 ycopy(c, n).start()
             else:
-                own[c - n_send, n] = part
+                own[c, n] = part
             return x
 
         lax.fori_loop(0, n_col, column, 0)
 
-    lead = min(2, n_ch - 1)
-    for c in range(lead + 1):
-        finish(c)
-    forward(0)
-    for c in range(lead + 1, n_ch):
+    for c in range(n_ch):
         finish(c)
     for cp in wloads:
         cp.wait()
+    near()
     for c in range(n_ch):
-        if c + 1 < n_ch and c > 0:
-            forward(c + 1)
-        multiply(c)
-        if c == 0 and n_ch > 1:
-            forward(1)
+        forward(c)
+        for d in range(1, xs):
+            far(c, ((tx + d) % xs) * 2 + core, False)
+        for d in range(1, xs):
+            who = ((tx + d) % xs) * 2 + (1 - core)
+            gcopy(c, who, mate, 0).wait_recv()
+            far(c, who, d == xs - 1)
 
     for s in range(sub):
         for n in range(n_col):
-            total = own[s, n]
+            total = own[n_send + s, n]
             for d in range(1, n_kv):
                 c = (d - 1) * sub + s
                 ycopy(c, n).wait_recv()
@@ -262,7 +280,7 @@
             pltpu.VMEM((n_ch, n_tok, heads, ch, HEAD_SIZE), bf),
             pltpu.VMEM((n_send, n_col, ch, ct), bf),
             pltpu.VMEM((n_send, n_col, ch, ct), bf),
-            pltpu.VMEM((sub, n_col, ch, ct), f32),
+            pltpu.VMEM((n_ch, n_col, ch, ct), f32),
             dma((2 + heads,)),
             dma((n_col,)),
             dma((reach,)),

time: 36.6 us -> 36.4 us (level)
  the two profiles are of different devices: /device:TPU:17 before, /device:TPU:18 now
where the time goes in v2:
time: 36.4 us; the launch traced here: 36.2 us
  Pallas kernels  31.7 us (87%)
  local copies, waits for them, and re-layouts  4.43 us (12%)
    pallas_call x1, Pallas kernels, per_device(): pl.pallas_call(functools.partial(kernel, dims), out_shape=jax.ShapeDtypeS...  31.7 us
    unnamed x7, local copies, waits for them, and re-layouts  3.74 us

profile of v2, /device:TPU:18, one launch (start us, length us, event | category | flops | bytes accessed | tf_op | source)
XLA Modules:
  0.0 36.2 jit_solution(16993747483914162169)
XLA Ops:
  0.0 0.7 %reshape.3.doc_ref = s32[4,256]{1,0:T(4,128)S(1)} reshape(s32[1024]{0:T(1024)} %param.8) | data formatting | bytes 8192 | tf_op jit(solution)/shard_map/reshape | solution.py:297
  0.7 0.0 copy-start
  0.7 1.0 %copy-done = bf16[256,1024]{1,0:T(8,128)(2,1)S(1)} copy-done((bf16[256,1024]{1,0:T(8,128)(2,1)S(1)}, bf16[256,1024]{1,0:T(8,128)(2,1)}, u32[]{:S(2)}) %copy-start) | copy-done | bytes 524312
  1.7 0.0 copy-start.1
  1.7 0.9 %copy-done.1 = bf16[256,512]{1,0:T(8,128)(2,1)S(1)} copy-done((bf16[256,512]{1,0:T(8,128)(2,1)S(1)}, bf16[256,512]{1,0:T(8,128)(2,1)}, u32[]{:S(2)}) %copy-start.1) | copy-done | bytes 262168
  2.7 0.0 copy-start.2
  2.7 0.9 %copy-done.2 = bf16[256,512]{1,0:T(8,128)(2,1)S(1)} copy-done((bf16[256,512]{1,0:T(8,128)(2,1)S(1)}, bf16[256,512]{1,0:T(8,128)(2,1)}, u32[]{:S(2)}) %copy-start.2) | copy-done | bytes 262168
  3.6 31.7 %shard_map.55 = bf16[128,2048]{1,0:T(8,128)(2,1)S(1)} custom-call(s32[4,256]{1,0:T(4,128)S(1)} %reshape.3.doc_ref, bf16[256,1024]{1,0:T(8,128)(2,1)S(1)} %copy-done, bf16[256,512]{1,0:T(8,128)(2,1)S(1)} %copy-done.1, bf16[256,512]{1,0:T(8,128)(2,1)S(1)} %copy-done.2, bf16[4096,2048]{1,0:T(8,128)(2,1)} %w_hbm.1), custom_call_target="tpu_custom_call" | custom-call | flops 5100273664 | bytes 16777216 | tf_op jit(solution)/shard_map/pallas_call | solution.py:269
  35.4 0.8 %copy.7 = bf16[128,2048]{1,0:T(8,128)(2,1)} copy(bf16[128,2048]{1,0:T(8,128)(2,1)S(1)} %shard_map.55) | data formatting | bytes 1048576
Async XLA Ops:
  0.7 1.0 %copy-start = (bf16[256,1024]{1,0:T(8,128)(2,1)S(1)}, bf16[256,1024]{1,0:T(8,128)(2,1)}, u32[]{:S(2)}) copy-start(bf16[256,1024]{1,0:T(8,128)(2,1)} %q_hbm.1) | copy-start | bytes 1572868
  1.7 0.9 %copy-start.1 = (bf16[256,512]{1,0:T(8,128)(2,1)S(1)}, bf16[256,512]{1,0:T(8,128)(2,1)}, u32[]{:S(2)}) copy-start(bf16[256,512]{1,0:T(8,128)(2,1)} %k_hbm.1) | copy-start | bytes 786436
  2.7 0.9 %copy-start.2 = (bf16[256,512]{1,0:T(8,128)(2,1)S(1)}, bf16[256,512]{1,0:T(8,128)(2,1)}, u32[]{:S(2)}) copy-start(bf16[256,512]{1,0:T(8,128)(2,1)} %v_hbm.1) | copy-start | bytes 786436

commit v3 on v2

--- a/solution.py
+++ b/solution.py
@@ -217,10 +217,12 @@
     for cp in wloads:
         cp.wait()
     near()
+    forward(0)
     for c in range(n_ch):
-        forward(c)
         for d in range(1, xs):
             far(c, ((tx + d) % xs) * 2 + core, False)
+        if c + 1 < n_ch:
+            forward(c + 1)
         for d in range(1, xs):
             who = ((tx + d) % xs) * 2 + (1 - core)
             gcopy(c, who, mate, 0).wait_recv()

time: 36.4 us -> 36.4 us (level)
  no operation moved by 1% of the time
where the time goes in v3:
time: 36.4 us; the launch traced here: 36.2 us
  Pallas kernels  31.7 us (87%)
  local copies, waits for them, and re-layouts  4.43 us (12%)
    pallas_call x1, Pallas kernels, per_device(): pl.pallas_call(functools.partial(kernel, dims), out_shape=jax.ShapeDtypeS...  31.7 us
    unnamed x7, local copies, waits for them, and re-layouts  3.74 us

profile of v3, /device:TPU:18, one launch (start us, length us, event | category | flops | bytes accessed | tf_op | source)
XLA Modules:
  0.0 36.2 jit_solution(14557707021848375352)
XLA Ops:
  0.0 0.7 %reshape.3.doc_ref = s32[4,256]{1,0:T(4,128)S(1)} reshape(s32[1024]{0:T(1024)} %param.8) | data formatting | bytes 8192 | tf_op jit(solution)/shard_map/reshape | solution.py:299
  0.7 0.0 copy-start
  0.7 1.0 %copy-done = bf16[256,1024]{1,0:T(8,128)(2,1)S(1)} copy-done((bf16[256,1024]{1,0:T(8,128)(2,1)S(1)}, bf16[256,1024]{1,0:T(8,128)(2,1)}, u32[]{:S(2)}) %copy-start) | copy-done | bytes 524312
  1.7 0.0 copy-start.1
  1.7 0.9 %copy-done.1 = bf16[256,512]{1,0:T(8,128)(2,1)S(1)} copy-done((bf16[256,512]{1,0:T(8,128)(2,1)S(1)}, bf16[256,512]{1,0:T(8,128)(2,1)}, u32[]{:S(2)}) %copy-start.1) | copy-done | bytes 262168
  2.7 0.0 copy-start.2
  2.7 0.9 %copy-done.2 = bf16[256,512]{1,0:T(8,128)(2,1)S(1)} copy-done((bf16[256,512]{1,0:T(8,128)(2,1)S(1)}, bf16[256,512]{1,0:T(8,128)(2,1)}, u32[]{:S(2)}) %copy-start.2) | copy-done | bytes 262168
  3.6 31.7 %shard_map.55 = bf16[128,2048]{1,0:T(8,128)(2,1)S(1)} custom-call(s32[4,256]{1,0:T(4,128)S(1)} %reshape.3.doc_ref, bf16[256,1024]{1,0:T(8,128)(2,1)S(1)} %copy-done, bf16[256,512]{1,0:T(8,128)(2,1)S(1)} %copy-done.1, bf16[256,512]{1,0:T(8,128)(2,1)S(1)} %copy-done.2, bf16[4096,2048]{1,0:T(8,128)(2,1)} %w_hbm.1), custom_call_target="tpu_custom_call" | custom-call | flops 5100273664 | bytes 16777216 | tf_op jit(solution)/shard_map/pallas_call | solution.py:271
  35.4 0.8 %copy.7 = bf16[128,2048]{1,0:T(8,128)(2,1)} copy(bf16[128,2048]{1,0:T(8,128)(2,1)S(1)} %shard_map.55) | data formatting | bytes 1048576
Async XLA Ops:
  0.7 1.0 %copy-start = (bf16[256,1024]{1,0:T(8,128)(2,1)S(1)}, bf16[256,1024]{1,0:T(8,128)(2,1)}, u32[]{:S(2)}) copy-start(bf16[256,1024]{1,0:T(8,128)(2,1)} %q_hbm.1) | copy-start | bytes 1572868
  1.7 0.9 %copy-start.1 = (bf16[256,512]{1,0:T(8,128)(2,1)S(1)}, bf16[256,512]{1,0:T(8,128)(2,1)}, u32[]{:S(2)}) copy-start(bf16[256,512]{1,0:T(8,128)(2,1)} %k_hbm.1) | copy-start | bytes 786436
  2.7 0.9 %copy-start.2 = (bf16[256,512]{1,0:T(8,128)(2,1)S(1)}, bf16[256,512]{1,0:T(8,128)(2,1)}, u32[]{:S(2)}) copy-start(bf16[256,512]{1,0:T(8,128)(2,1)} %v_hbm.1) | copy-start | bytes 786436
